TPU v7x, 32 devices: a whole 2x2x4 slice. The times are simulated.
32 devices in a mesh: dp: 4 (over y, core), fsdp: 4 (over z), tensor: 2 (over x).
Axes of the slice: x: 2, y: 2, z: 4, core: 2. Of those that a mesh axis runs over, the one named last changes fastest.
Arguments:
- tokens: bfloat16 [32, 128, 4096], P(('dp', 'fsdp')), may hold values from -6 to 6
- send_flags: int32 [4, 4], replicated, may hold values from 0 to 1
- doc_lengths: int32 [32, 4], replicated, may hold values from 1 to 64, 128 in all within a row
- cotangent: bfloat16 [32, 128, 8192], P(('dp', 'fsdp')), may hold values from -6 to 6
- w_x: bfloat16 [4096, 8192], P(None, ('fsdp', 'tensor')), may hold values from -0.09375 to 0.09375
- w_z: bfloat16 [4096, 8192], P(None, ('fsdp', 'tensor')), may hold values from -0.09375 to 0.09375
- w_dt: bfloat16 [4096, 128], P(None, ('fsdp', 'tensor')), may hold values from -0.09375 to 0.09375
- w_bc: bfloat16 [4096, 256], replicated, may hold values from -0.09375 to 0.09375
- conv_w: float32 [4, 8192], P(None, ('fsdp', 'tensor')), may hold values from -0.5 to 0.5
- conv_b: float32 [8192], P(('fsdp', 'tensor')), may hold values from -0.5 to 0.5
- norm_gain: float32 [8192], P(('fsdp', 'tensor')), may hold values from 0.5 to 1.5
- a_log: float32 [128], P(('fsdp', 'tensor')), may hold values from 0 to 2.77
- dt_bias: float32 [128], P(('fsdp', 'tensor')), may hold values from -6.9 to -2.3
- skip_scale: float32 [128], P(('fsdp', 'tensor')), may hold values from 0.5 to 1.5
Outputs:
- grad_w_x: float32 [4096, 8192], P('dp', ('fsdp', 'tensor'))
- grad_w_z: float32 [4096, 8192], P('dp', ('fsdp', 'tensor'))
- grad_w_dt: float32 [4096, 128], P('dp', ('fsdp', 'tensor'))
- grad_channel: float32 [6, 8192], P(None, ('fsdp', 'tensor'))
- grad_head: float32 [3, 128], P(None, ('fsdp', 'tensor'))
Inputs may be any that keep to these rules, and one draw needn't show every extreme that they name: `send_flags`: each flag is 0 or 1; slots of a device beyond its live count hold values that no output reads. `doc_lengths`: each block's lengths sum to 128, and the largest is exactly 64.
All inputs are finite; a program needn't handle non-finite values.
Results may differ from a plain program's by a relative error of at most 0.009.
Values may be sent and summed in bfloat16 or wider, within the bound.
No kernel may reach another device: no remote copies, remote signals or barrier semaphores. Data moves between devices by JAX's collectives and lax.ppermute only.
A program may use at most 128 MiB of HBM per device.

v0:
```python
import jax
import jax.numpy as jnp
from jax import lax
from jax.experimental import pallas as pl
from jax.experimental.pallas import tpu as pltpu
from jax.sharding import PartitionSpec as P

NORM_GROUP = 512
PAIR = 128
CHUNKS = 2
F32 = jnp.float32
BF16 = jnp.bfloat16


def split_two(v):
    hi = v.astype(BF16)
    return hi, (v - hi.astype(F32)).astype(BF16)


def split_three(v):
    hi = v.astype(BF16)
    rest = v - hi.astype(F32)
    mid = rest.astype(BF16)
    return hi, mid, (rest - mid.astype(F32)).astype(BF16)


def dot_nn(a, b):
    return lax.dot_general(a, b, (((1,), (0,)), ((), ())), preferred_element_type=F32)


def dot_nt(a, b):
    return lax.dot_general(a, b, (((1,), (1,)), ((), ())), preferred_element_type=F32)


def dot_tn(a, b):
    return lax.dot_general(a, b, (((0,), (0,)), ((), ())), preferred_element_type=F32)


def exact_rows(rows, ones):
    n = rows.shape[0]
    got = dot_nn(jnp.concatenate(split_three(rows), axis=0), ones)
    return got[:n] + got[n : 2 * n] + got[2 * n :]


def scan_kernel(
    ends_ref, px_ref, pz_ref, pdt_ref, cot_ref, bc_ref,
    cw_ref, cb_ref, gain_ref, skipc_ref, alog_ref, dtb_ref,
    gpre_ref, gpdt_ref, gch_ref, gh_ref,
):
    block = pl.program_id(1)
    length = px_ref.shape[1]
    group = px_ref.shape[2]
    taps = cw_ref.shape[0]
    states = bc_ref.shape[2] // 2
    heads = pdt_ref.shape[2]
    head_dim = group // heads
    pairs = group // PAIR
    docs = ends_ref.shape[1]

    row = lax.broadcasted_iota(jnp.int32, (length, length), 0)
    col = lax.broadcasted_iota(jnp.int32, (length, length), 1)
    start_row = jnp.zeros((length, length), jnp.int32)
    start_col = jnp.zeros((length, length), jnp.int32)
    for k in range(docs):
        end = ends_ref[block, k]
        start_row = jnp.where(row >= end, end, start_row)
        start_col = jnp.where(col >= end, end, start_col)
    inside = (row >= col) & (start_row == start_col)
    offset = (row - start_row)[:, :PAIR]
    near = [None] + [(offset >= j).astype(F32) for j in range(1, taps)]
    low = lax.broadcasted_iota(jnp.int32, (length, PAIR), 1) < head_dim
    upto = (row <= col).astype(BF16)

    bmat = bc_ref[0, :, :states]
    cmat = bc_ref[0, :, states:]
    scores = dot_nt(cmat, bmat)

    decay = -jnp.exp(alog_ref[0])
    raw = pdt_ref[0, 0] + dtb_ref[0]
    soft = jnp.exp(-jnp.abs(raw))
    step = jnp.maximum(raw, 0.0) + jnp.log1p(soft)
    dstep = jnp.where(raw >= 0.0, 1.0, soft) / (1.0 + soft)
    level = exact_rows(step * decay, upto)
    both = jnp.concatenate(
        [step, level, jnp.zeros((length - 2 * heads, length), F32)], axis=0
    ).T

    kept = []
    square_sum = jnp.zeros((length, PAIR), F32)
    cross_sum = jnp.zeros((length, PAIR), F32)
    for k in range(pairs):
        at = slice(k * PAIR, (k + 1) * PAIR)
        x = px_ref[0, :, at]
        back = [x] + [near[j] * pltpu.roll(x, j, 0) for j in range(1, taps)]
        s = cb_ref[:, at]
        for j in range(taps):
            s = s + cw_ref[taps - 1 - j : taps - j, at] * back[j]
        sig = jax.nn.sigmoid(s)
        u = s * sig
        dsilu = sig * (1.0 + s * (1.0 - sig))
        spread = []
        for h in (2 * k, 2 * k + 1):
            gap = both[:, heads + h : heads + h + 1] - level[h : h + 1, :]
            spread.append((jnp.exp(jnp.where(inside, gap, -1e30)) * scores).astype(BF16))
        step_wide = jnp.where(low, both[:, 2 * k : 2 * k + 1], both[:, 2 * k + 1 : 2 * k + 2])
        ud = (step_wide * u).astype(BF16).astype(F32)
        zero = jnp.zeros_like(ud)
        udc = jnp.concatenate([jnp.where(low, ud, zero), jnp.where(low, zero, ud)], axis=0).astype(BF16)
        mix = dot_nn(jnp.concatenate(spread, axis=1), udc)
        y = mix + skipc_ref[:, at] * u
        z = pz_ref[0, :, at]
        zsig = jax.nn.sigmoid(z)
        zs = z * zsig
        v = y * zs
        dn = cot_ref[0, :, at].astype(F32) * gain_ref[:, at]
        square_sum = square_sum + v * v
        cross_sum = cross_sum + dn * v
        kept.append((back, u, ud, dsilu, jnp.concatenate(spread, axis=0), step_wide, mix, y, z, zsig, zs, v, dn))

    inv = lax.rsqrt(jnp.sum(square_sum, axis=1, keepdims=True) * (1.0 / group) + 1e-05)
    lean = inv * inv * jnp.sum(cross_sum, axis=1, keepdims=True) * (1.0 / group)

    channel_rows = []
    use_parts = []
    mix_parts = []
    skip_parts = []
    for k in range(pairs):
        at = slice(k * PAIR, (k + 1) * PAIR)
        back, u, ud, dsilu, spread, step_wide, mix, y, z, zsig, zs, v, dn = kept[k]
        dgain = jnp.sum(cot_ref[0, :, at].astype(F32) * (v * inv), axis=0, keepdims=True)
        dv = inv * (dn - v * lean)
        dy = dv * zs
        dz = dv * y * (zsig * (1.0 + z * (1.0 - zsig)))
        gpre_ref[1, 0, :, at] = dz.astype(BF16)
        dyr = dy.astype(BF16).astype(F32)
        zero = jnp.zeros_like(dy)
        dyc = jnp.concatenate([jnp.where(low, dyr, zero), jnp.where(low, zero, dyr)], axis=0).astype(BF16)
        turned = dot_tn(spread, dyc)
        du = step_wide * turned + skipc_ref[:, at] * dy
        use_parts.append(u * turned)
        mix_parts.append(dyr * mix - ud * turned)
        skip_parts.append(jnp.sum(dy * u, axis=0, keepdims=True))
        ds = du * dsilu
        rows = []
        dx = cw_ref[taps - 1 : taps, at] * ds
        for j in range(taps - 1, 0, -1):
            rows.append(jnp.sum(ds * back[j], axis=0, keepdims=True))
            dx = dx + cw_ref[taps - 1 - j : taps - j, at] * pltpu.roll(near[j] * ds, length - j, 0)
        rows.append(jnp.sum(ds * back[0], axis=0, keepdims=True))
        rows.append(jnp.sum(ds, axis=0, keepdims=True))
        rows.append(dgain)
        gpre_ref[0, 0, :, at] = dx.astype(BF16)
        channel_rows.append(jnp.concatenate(rows, axis=0))
    channel = jnp.concatenate(channel_rows, axis=1)

    of_head = (
        lax.broadcasted_iota(jnp.int32, (heads, group), 1) // head_dim
        == lax.broadcasted_iota(jnp.int32, (heads, group), 0)
    ).astype(BF16)
    use_hi, use_lo = split_two(jnp.concatenate(use_parts, axis=1))
    use_sum = dot_nt(of_head, use_hi) + dot_nt(of_head, use_lo)
    mix_hi, mix_lo = split_two(jnp.concatenate(mix_parts, axis=1))
    mix_sum = dot_nt(of_head, mix_hi) + dot_nt(of_head, mix_lo)
    after = exact_rows(mix_sum, (row >= col).astype(BF16))
    dalog = jnp.sum(step * after, axis=1, keepdims=True) * decay
    draw = (use_sum + decay * after) * dstep
    gpdt_ref[0, 0] = draw
    ddtb = jnp.sum(draw, axis=1, keepdims=True)
    skip_row = jnp.concatenate(skip_parts, axis=1)
    dskip = jnp.sum(jnp.where(of_head > 0, skip_row, 0.0), axis=1, keepdims=True)
    head = jnp.concatenate([dalog, ddtb, dskip], axis=1)

    @pl.when(block == 0)
    def _():
        gch_ref[...] = channel
        gh_ref[0] = head

    @pl.when(block > 0)
    def _():
        gch_ref[...] += channel
        gh_ref[0] += head


def scan_backward(ends, px, pz, pdt, cot, bc, conv_w, conv_b, norm_gain, skip_chan, a_log, dt_bias):
    blocks, length, channels = px.shape
    groups, _, heads, _ = pdt.shape
    taps = conv_w.shape[0]
    wide = channels // groups
    per_block = pl.BlockSpec((1, length, wide), lambda g, b: (b, 0, g))
    per_group = lambda rows: pl.BlockSpec((rows, wide), lambda g, b: (0, g))
    head_spec = pl.BlockSpec((1, heads, 1), lambda g, b: (g, 0, 0))
    return pl.pallas_call(
        scan_kernel,
        grid=(groups, blocks),
        in_specs=[
            pl.BlockSpec(memory_space=pltpu.SMEM),
            per_block, per_block,
            pl.BlockSpec((1, 1, heads, length), lambda g, b: (g, b, 0, 0)),
            per_block,
            pl.BlockSpec((1, length, bc.shape[2]), lambda g, b: (b, 0, 0)),
            per_group(taps), per_group(1), per_group(1), per_group(1),
            head_spec, head_spec,
        ],
        out_specs=[
            pl.BlockSpec((2, 1, length, wide), lambda g, b: (0, b, 0, g)),
            pl.BlockSpec((1, 1, heads, length), lambda g, b: (g, b, 0, 0)),
            per_group(taps + 2),
            pl.BlockSpec((1, heads, 3), lambda g, b: (g, 0, 0)),
        ],
        out_shape=[
            jax.ShapeDtypeStruct((2, blocks, length, channels), BF16),
            jax.ShapeDtypeStruct(pdt.shape, F32),
            jax.ShapeDtypeStruct((taps + 2, channels), F32),
            jax.ShapeDtypeStruct((groups, heads, 3), F32),
        ],
        compiler_params=pltpu.CompilerParams(vmem_limit_bytes=32 * 2**20),
        cost_estimate=pl.CostEstimate(
            flops=400 * blocks * length * channels,
            bytes_accessed=18 * blocks * length * channels,
            transcendentals=10 * blocks * length * channels,
        ),
    )(
        ends, px, pz, pdt, cot, bc, conv_w, conv_b[None], norm_gain[None], skip_chan[None],
        a_log.reshape(groups, heads, 1), dt_bias.reshape(groups, heads, 1),
    )


def xor_pairs(size, by):
    return [(i, i ^ by) for i in range(size)]


def shifted(shard, axis, by):
    size = lax.axis_size(axis)
    return lax.ppermute(shard, axis, [(i, (i + by) % size) for i in range(size)])


def swapped(shard, axis, by):
    return lax.ppermute(shard, axis, xor_pairs(lax.axis_size(axis), by))


def after(value, *others):
    return lax.optimization_barrier((value, *others))[0]


def tree_sum(parts):
    while len(parts) > 1:
        parts = [a + b for a, b in zip(parts[0::2], parts[1::2], strict=True)]
    return parts[0]


def per_device(
    tokens,
    send_flags,
    doc_lengths,
    cotangent,
    w_x,
    w_z,
    w_dt,
    w_bc,
    conv_w,
    conv_b,
    norm_gain,
    a_log,
    dt_bias,
    skip_scale,
):
    dp_count = lax.axis_size("dp")
    fsdp_count = lax.axis_size("fsdp")
    pair_count = lax.axis_size("tensor")
    dp_index = lax.axis_index("dp")
    column = lax.axis_index("fsdp")
    member = lax.axis_index("tensor")
    slots, length, width = tokens.shape
    half = length // pair_count
    chan = w_x.shape[1]
    head_count = w_dt.shape[1]
    groups = chan // NORM_GROUP
    taps = conv_w.shape[0]
    piece = width // dp_count
    zero = jnp.zeros((), jnp.int32)

    before = (dp_index + dp_count - 1) % dp_count
    earlier = (dp_index + dp_count - 2) % dp_count
    came = send_flags[before, column] == 1
    own_send = 1 - send_flags[before, column]

    def in_order(mine, other):
        first = jnp.where(member == 0, mine, other)
        second = jnp.where(member == 0, other, mine)
        return jnp.concatenate((first, second), axis=-2)

    def across(own):
        held = [own]
        for k in range(1, fsdp_count):
            low = k & -k
            held.append(swapped(held[k ^ low], "fsdp", low))
        return held

    def half_rows(slot):
        return lax.dynamic_slice(tokens, (slot, member * half, zero), (1, half, width))[0]

    mine_x = jnp.where(came, shifted(half_rows(own_send), "dp", 1), half_rows(zero))
    mine = across(mine_x)
    x_blocks = [in_order(part, swapped(part, "tensor", 1)) for part in mine]

    held_d = after(cotangent, mine_x)

    def slabs(slot):
        return jnp.stack(
            [
                lax.dynamic_slice(held_d, (slot, zero, (f * pair_count + member) * chan), (1, length, chan))[0]
                for f in range(fsdp_count)
            ]
        )

    mine_d = jnp.where(came, shifted(slabs(own_send), "dp", 1), slabs(zero))
    d_blocks = []
    for k in range(fsdp_count):
        part = lax.dynamic_index_in_dim(mine_d, column ^ k, 0, keepdims=False)
        d_blocks.append(swapped(part, "fsdp", k) if k else part)

    def columns_for(rows, m):
        at = (zero,) * (rows.ndim - 1) + ((dp_index ^ m) * piece,)
        return lax.dynamic_slice(rows, at, rows.shape[:-1] + (piece,))

    held_x = after(mine_x, mine_d)
    far_x = jnp.stack([swapped(columns_for(held_x, m), "dp", m) for m in range(2, dp_count)])
    far_x = after(far_x, d_blocks[-1], mine[-1])
    far_x = jnp.stack(across(far_x))
    far_x = in_order(far_x, swapped(far_x, "tensor", 1))

    columns = column ^ jnp.arange(fsdp_count, dtype=jnp.int32)
    picks = jnp.where(
        send_flags[before][columns] == 1,
        (before * fsdp_count + columns) * slots + 1 - send_flags[earlier][columns],
        (dp_index * fsdp_count + columns) * slots,
    )
    sizes = doc_lengths[picks]
    ends = [sizes[:, 0]]
    for k in range(1, sizes.shape[1] - 1):
        ends.append(ends[-1] + sizes[:, k])
    ends = jnp.stack(ends, axis=1)
    skip_chan = jnp.repeat(skip_scale, chan // head_count)

    per_chunk = max(1, fsdp_count // CHUNKS)
    x_parts = [[] for _ in range(dp_count)]
    g_parts = [[] for _ in range(dp_count)]
    dt_parts = []
    channel_parts = []
    head_parts = []
    for first in range(0, fsdp_count, per_chunk):
        last = first + per_chunk
        xs = jnp.concatenate(x_blocks[first:last], axis=0)
        cot = jnp.stack(d_blocks[first:last])
        px = jnp.dot(xs, w_x, preferred_element_type=F32).reshape(per_chunk, length, chan)
        pz = jnp.dot(xs, w_z, preferred_element_type=F32).reshape(per_chunk, length, chan)
        bc = jnp.dot(xs, w_bc, preferred_element_type=F32).astype(BF16)
        bc = bc.reshape(per_chunk, length, w_bc.shape[1])
        pdt = lax.dot_general(w_dt, xs, (((0,), (1,)), ((), ())), preferred_element_type=F32)
        pdt = pdt.reshape(groups, head_count // groups, per_chunk, length).transpose(0, 2, 1, 3)
        gpre, gpdt, gch, gh = scan_backward(
            ends[first:last], px, pz, pdt, cot, bc,
            conv_w, conv_b, norm_gain, skip_chan, a_log, dt_bias,
        )
        dt_parts.append(gpdt.transpose(1, 0, 2, 3).reshape(per_chunk, head_count, length))
        channel_parts.append(gch)
        head_parts.append(gh)
        gpre = gpre.reshape(2, per_chunk * length, chan)
        for m in range(0, dp_count, 2):
            got = swapped(gpre, "dp", m) if m else gpre
            g_parts[m].append(got)
            g_parts[m + 1].append(swapped(got, "dp", 1))
        x_parts[0].append(columns_for(xs, 0))
        x_parts[1].append(swapped(columns_for(xs, 1), "dp", 1))
        for m in range(2, dp_count):
            x_parts[m].append(far_x[first:last, m - 2].reshape(-1, piece))

    gpdt = jnp.concatenate(dt_parts, axis=0).reshape(-1, chan)
    rows = [gpdt, sum(channel_parts[1:], channel_parts[0])]
    heads = sum(head_parts[1:], head_parts[0]).reshape(head_count, 3).T
    rows.append(jnp.pad(heads.reshape(1, -1), ((0, 0), (0, chan - 3 * head_count))))
    packed = jnp.concatenate(rows, axis=0)
    packs = [packed if m == 0 else swapped(packed, "dp", m) for m in range(dp_count)]
    dt_rows = gpdt.shape[0]
    small = tree_sum([p[dt_rows:] for p in packs])
    channel_sum = small[: taps + 2]
    head_sum = small[taps + 2, : 3 * head_count].reshape(3, head_count)

    def product(ms, which):
        x_all = jnp.concatenate([p for m in ms for p in x_parts[m]], axis=0)
        g_all = jnp.concatenate([p[which] for m in ms for p in g_parts[m]], axis=0)
        return lax.dot_general(x_all, g_all, (((0,), (0,)), ((), ())), preferred_element_type=F32)

    near = tuple(range(2))
    far = tuple(range(2, dp_count))
    grad_x = product(near, 0) + product(far, 0)
    grad_z = product(near, 1) + product(far, 1)
    x_all = jnp.concatenate([p for parts in x_parts for p in parts], axis=0)
    dt_all = jnp.concatenate([p[:dt_rows].reshape(-1, head_count, length) for p in packs], axis=0)
    dt_all = dt_all.astype(BF16).transpose(1, 0, 2).reshape(head_count, -1)
    grad_dt = lax.dot_general(x_all, dt_all, (((0,), (1,)), ((), ())), preferred_element_type=F32)
    return grad_x, grad_z, grad_dt, channel_sum, head_sum


def solution(mesh):
    split = ("fsdp", "tensor")
    placed = (
        P(("dp", "fsdp"), None, None),
        P(),
        P(),
        P(("dp", "fsdp"), None, None),
        P(None, split),
        P(None, split),
        P(None, split),
        P(),
        P(None, split),
        P(split),
        P(split),
        P(split),
        P(split),
        P(split),
    )
    return jax.shard_map(
        per_device,
        mesh=mesh,
        in_specs=placed,
        out_specs=(P("dp", split), P("dp", split), P("dp", split), P(None, split), P(None, split)),
        check_vma=False,
    )
```

profile of v0, /device:TPU:1, one launch (start us, length us, event | category | flops | bytes accessed | tf_op | source)
XLA Modules:
  0.0 184.2 jit_solution(2788600367115292438)
XLA Ops:
  4.5 2.7 %collective-permute-start = (bf16[64,4096]{1,0:T(8,128)(2,1)S(1)}, bf16[64,4096]{1,0:T(8,128)(2,1)S(1)}, u32[]{:S(2)}, u32[]{:S(2)}) collective-permute-start(bf16[64,4096]{1,0:T(8,128)(2,1)S(1)} %dynamic-slice_bitcast_fusion), channel_id=1, source_target_pairs={{0,8},{8,16},{16,24},{24,0},{1,9},{9,17},{17,25},{25,1},{2,10},{10... | collective-permute-start | bytes 1572872 | tf_op jit(solution)/shard_map/ppermute | solution.py:234
  19.3 2.7 %constant_dynamic-slice_fusion.6 = (bf16[1,128,1024]{2,1,0:T(8,128)(2,1)S(1)}, bf16[1,128,1024]{2,1,0:T(8,128)(2,1)S(1)}, bf16[1,128,1024]{2,1,0:T(8,128)(2,1)S(...) fusion(bf16[2,128,8192]{2,1,0:T(8,128)(2,1)} %param.17, ...), kind=kLoop, calls=%fused_computation.116 | loop fusion | bytes 4194324 | tf_op jit(solution)/shard_map/dynamic_slice | solution.py:311
  23.1 3.3 %collective-permute-start.10 = (bf16[4,128,1024]{2,1,0:T(8,128)(2,1)}, bf16[4,128,1024]{2,1,0:T(8,128)(2,1)}, u32[]{:S(2)}, u32[]{:S(2)}) collective-permute-start(bf16[4,128,1024]{2,1,0:T(8,128)(2,1)} %pad_maximum_fusion.4), channel_id=1, source_target_pairs={{0,8},{8,16},{16,24},{24,0},{1,9},{9,17},{17,25},{25,1},{2,10},{10... | collective-permute-start | bytes 3145736 | tf_op jit(solution)/shard_map/ppermute | solution.py:234
  26.8 10.2 %collective-permute-done.4 = bf16[64,4096]{1,0:T(8,128)(2,1)} collective-permute-done((bf16[64,4096]{1,0:T(8,128)(2,1)S(1)}, bf16[64,4096]{1,0:T(8,128)(2,1)}, u32[]{:S(2)}, u32[]{:S(2)}) %collective-permute-start.4) | collective-permute-done | bytes 524320 | tf_op jit(solution)/shard_map/ppermute | solution.py:238
  38.2 3.3 %collective-permute-start.6 = (bf16[64,4096]{1,0:T(8,128)(2,1)}, bf16[64,4096]{1,0:T(8,128)(2,1)S(1)}, u32[]{:S(2)}, u32[]{:S(2)}) collective-permute-start(bf16[64,4096]{1,0:T(8,128)(2,1)} %collective-permute-done.4), channel_id=1, source_target_pairs={{0,2},{2,0},{4,6},{6,4},{1,3},{3,1},{5,7},{7,5},{8,10},{10,8},{12,... | collective-permute-start | bytes 1572872 | tf_op jit(solution)/shard_map/ppermute | solution.py:238
  44.7 10.5 %collective-permute-done.3 = bf16[64,4096]{1,0:T(8,128)(2,1)S(1)} collective-permute-done((bf16[64,4096]{1,0:T(8,128)(2,1)}, bf16[64,4096]{1,0:T(8,128)(2,1)S(1)}, u32[]{:S(2)}, u32[]{:S(2)}) %collective-permute-start.3) | collective-permute-done | bytes 524320 | tf_op jit(solution)/shard_map/ppermute | solution.py:238
  55.2 6.7 %collective-permute-start.17 = (bf16[64,1024]{1,0:T(8,128)(2,1)S(1)}, bf16[64,1024]{1,0:T(8,128)(2,1)S(1)}, u32[]{:S(2)}, u32[]{:S(2)}) collective-permute-start(bf16[64,1024]{1,0:T(8,128)(2,1)S(1)} %get-tuple-element.78), channel_id=1, source_target_pairs={{0,24},{8,16},{16,8},{24,0},{1,25},{9,17},{17,9},{25,1},{2,26},{10... | collective-permute-start | bytes 393224 | tf_op jit(solution)/shard_map/ppermute | solution.py:238
  63.2 5.9 %fusion.58 = f32[256,1024]{1,0:T(8,128)S(1)} fusion(bf16[256,4096]{1,0:T(8,128)(2,1)S(1)} %pad_maximum_fusion, bf16[4096,1024]{1,0:T(8,128)(2,1)} %param.18), kind=kOutput, calls=%fused_computation.151 | convolution fusion | flops 2147483648 | bytes 11534336 | tf_op jit(solution)/shard_map/dot_general | solution.py:355
  69.1 2.3 %fusion.59 = f32[256,1024]{1,0:T(8,128)S(1)} fusion(bf16[256,4096]{1,0:T(8,128)(2,1)S(1)} %pad_maximum_fusion, bf16[4096,1024]{1,0:T(8,128)(2,1)S(1)} %bitcast.185), kind=kOutput, calls=%fused_computation.152 | convolution fusion | flops 2147483648 | bytes 11534336 | tf_op jit(solution)/shard_map/dot_general | solution.py:356
  73.2 3.4 %collective-permute-start.13 = (bf16[128,1024]{1,0:T(8,128)(2,1)S(1)}, bf16[128,1024]{1,0:T(8,128)(2,1)S(1)}, u32[]{:S(2)}, u32[]{:S(2)}) collective-permute-start(bf16[128,1024]{1,0:T(8,128)(2,1)S(1)} %get-tuple-element.66), channel_id=1, source_target_pairs={{0,6},{2,4},{4,2},{6,0},{1,7},{3,5},{5,3},{7,1},{8,14},{10,12},{12... | collective-permute-start | bytes 786440 | tf_op jit(solution)/shard_map/ppermute | solution.py:238
  79.8 2.8 %collective-permute-start.8 = (bf16[256,1024]{1,0:T(8,128)(2,1)}, bf16[256,1024]{1,0:T(8,128)(2,1)}, u32[]{:S(2)}, u32[]{:S(2)}) collective-permute-start(bf16[256,1024]{1,0:T(8,128)(2,1)} %get-tuple-element.48), channel_id=1, source_target_pairs={{0,8},{8,0},{16,24},{24,16},{1,9},{9,1},{17,25},{25,17},{2,10},{10... | collective-permute-start | bytes 1572872 | tf_op jit(solution)/shard_map/ppermute | solution.py:238
  82.7 12.2 %collective-permute-start.19 = (bf16[2,64,1024]{2,1,0:T(8,128)(2,1)S(1)}, bf16[2,64,1024]{2,1,0:T(8,128)(2,1)}, u32[]{:S(2)}, u32[]{:S(2)}) collective-permute-start(bf16[2,64,1024]{2,1,0:T(8,128)(2,1)S(1)} %pad_maximum_fusion.13), channel_id=1, source_target_pairs={{0,4},{2,6},{4,0},{6,2},{1,5},{3,7},{5,1},{7,3},{8,12},{10,14},{12... | collective-permute-start | bytes 786440 | tf_op jit(solution)/shard_map/ppermute | solution.py:238
  95.0 9.5 %shard_map.173 = (bf16[2,2,128,1024]{3,2,1,0:T(8,128)(2,1)S(1)}, f32[2,2,8,128]{3,2,1,0:T(8,128)S(1)}, f32[6,1024]{1,0:T(8,128)S(1)}, f32[2,8,3]{2,1,0:T(8,128)S(1)}) custom-call(s32[2,3]{1,0:T(2,128)S(1)} %get-tuple-element.79.ends_ref, f32[2,128,1024]{2,1,0:T(8,128)S(1)} %bitcast.148, f32[2,128,1024]{2,1,0:T(8,128)S(1)} %bitcast.149, ...), custom_call_target="tpu_custom_call" | custom-call | flops 104857600 | bytes 4718592 | tf_op jit(solution)/shard_map/pallas_call | solution.py:192
  110.2 2.3 %fusion.60 = f32[256,1024]{1,0:T(8,128)S(1)} fusion(bf16[256,4096]{1,0:T(8,128)(2,1)S(1)} %pad_maximum_fusion.1, bf16[4096,1024]{1,0:T(8,128)(2,1)S(1)} %bitcast.183), kind=kOutput, calls=%fused_computation.153 | convolution fusion | flops 2147483648 | bytes 11534336 | tf_op jit(solution)/shard_map/dot_general | solution.py:355
  112.5 2.3 %fusion.61 = f32[256,1024]{1,0:T(8,128)S(1)} fusion(bf16[256,4096]{1,0:T(8,128)(2,1)S(1)} %pad_maximum_fusion.1, bf16[4096,1024]{1,0:T(8,128)(2,1)S(1)} %bitcast.185), kind=kOutput, calls=%fused_computation.154 | convolution fusion | flops 2147483648 | bytes 11534336 | tf_op jit(solution)/shard_map/dot_general | solution.py:356
  116.2 9.5 %shard_map.174 = (bf16[2,2,128,1024]{3,2,1,0:T(8,128)(2,1)S(1)}, f32[2,2,8,128]{3,2,1,0:T(8,128)S(1)}, f32[6,1024]{1,0:T(8,128)S(1)}, f32[2,8,3]{2,1,0:T(8,128)S(1)}) custom-call(s32[2,3]{1,0:T(2,128)S(1)} %get-tuple-element.80.ends_ref, f32[2,128,1024]{2,1,0:T(8,128)S(1)} %bitcast.150, f32[2,128,1024]{2,1,0:T(8,128)S(1)} %bitcast.151, ...), custom_call_target="tpu_custom_call" | custom-call | flops 104857600 | bytes 4718592 | tf_op jit(solution)/shard_map/pallas_call | solution.py:192
  127.5 2.4 %constant_dynamic-update-slice_fusion.6 = (bf16[2048,1024]{1,0:T(8,128)(2,1)}, bf16[256,1024]{1,0:T(8,128)(2,1)}, bf16[256,1024]{1,0:T(8,128)(2,1)S(1)}) fusion(bf16[2048,1024]{1,0:T(8,128)(2,1)} %get-tuple-element.29, bf16[256,4096]{1,0:T(8,128)(2,1)} %copy-done.5, s32[]{:T(128)S(6)} %select_n.181, s32[]{:T(128)S(6)} %select_n.186), kind=kLoop, calls=%fused_computation.105 | loop fusion | bytes 2621448
  138.0 4.3 %collective-permute-done.20 = bf16[2,64,1024]{2,1,0:T(8,128)(2,1)S(1)} collective-permute-done((bf16[2,64,1024]{2,1,0:T(8,128)(2,1)}, bf16[2,64,1024]{2,1,0:T(8,128)(2,1)S(1)}, u32[]{:S(2)}, u32[]{:S(2)}) %collective-permute-start.20) | collective-permute-done | bytes 262176 | tf_op jit(solution)/shard_map/ppermute | solution.py:238
  150.5 9.4 %collective-permute-done.23 = bf16[2,256,1024]{2,1,0:T(8,128)(2,1)} collective-permute-done((bf16[2,256,1024]{2,1,0:T(8,128)(2,1)S(1)}, bf16[2,256,1024]{2,1,0:T(8,128)(2,1)}, u32[]{:S(2)}, u32[]{:S(2)}) %collective-permute-start.23) | collective-permute-done | bytes 1048608 | tf_op jit(solution)/shard_map/ppermute | solution.py:238
  159.9 2.4 %collective-permute-start.25 = (bf16[2,256,1024]{2,1,0:T(8,128)(2,1)}, bf16[2,256,1024]{2,1,0:T(8,128)(2,1)S(1)}, u32[]{:S(2)}, u32[]{:S(2)}) collective-permute-start(bf16[2,256,1024]{2,1,0:T(8,128)(2,1)} %collective-permute-done.23), channel_id=1, source_target_pairs={{0,8},{8,0},{16,24},{24,16},{1,9},{9,1},{17,25},{25,17},{2,10},{10... | collective-permute-start | bytes 3145736 | tf_op jit(solution)/shard_map/ppermute | solution.py:238
  163.7 3.7 %fusion.16 = f32[1024,1024]{1,0:T(8,128)S(1)} fusion(bf16[256,1024]{1,0:T(8,128)(2,1)S(1)} %get-tuple-element.63, bf16[256,1024]{1,0:T(8,128)(2,1)S(1)} %get-tuple-element.61, bf16[256,1024]{1,0:T(8,128)(2,1)S(1)} %bitcast.173, bf16[256,1024]{1,0:T(8,128)(2,1)S(1)} %bitcast.171, bf16[256,1024]{1,0:T(8,128)(2,1)} %collective-permute-done.9, ...), kind=kOutput, calls=%fused_computation.29 | convolution fusion | flops 2164260864 | bytes 8388608 | tf_op jit(solution)/shard_map/dot_general | solution.py:392
  167.5 3.7 %fusion = f32[1024,1024]{1,0:T(8,128)S(1)} fusion(bf16[256,1024]{1,0:T(8,128)(2,1)S(1)} %get-tuple-element.64, bf16[256,1024]{1,0:T(8,128)(2,1)S(1)} %get-tuple-element.62, bf16[256,1024]{1,0:T(8,128)(2,1)S(1)} %bitcast.172, bf16[256,1024]{1,0:T(8,128)(2,1)S(1)} %bitcast.170, bf16[256,1024]{1,0:T(8,128)(2,1)} %collective-permute-done.9, ...), kind=kOutput, calls=%fused_computation.12 | convolution fusion | flops 2164260864 | bytes 8388608 | tf_op jit(solution)/shard_map/dot_general | solution.py:392
  175.1 4.5 %fusion.32 = f32[1024,1024]{1,0:T(8,128)} fusion(f32[1024,1024]{1,0:T(8,128)S(1)} %fusion.16, bf16[256,1024]{1,0:T(8,128)(2,1)S(1)} %get-tuple-element.55, bf16[256,1024]{1,0:T(8,128)(2,1)S(1)} %get-tuple-element.53, bf16[256,1024]{1,0:T(8,128)(2,1)S(1)} %get-tuple-element.51, bf16[256,1024]{1,0:T(8,128)(2,1)S(1)} %get-tuple-element.49, ...), kind=kOutput, calls=%fused_computation.45 | convolution fusion | flops 2165309440 | bytes 12582912 | tf_op jit(solution)/shard_map/dot_general | solution.py:392
  179.7 4.5 %fusion.35 = f32[1024,1024]{1,0:T(8,128)} fusion(f32[1024,1024]{1,0:T(8,128)S(1)} %fusion, bf16[256,1024]{1,0:T(8,128)(2,1)S(1)} %get-tuple-element.56, bf16[256,1024]{1,0:T(8,128)(2,1)S(1)} %get-tuple-element.54, bf16[256,1024]{1,0:T(8,128)(2,1)S(1)} %get-tuple-element.52, bf16[256,1024]{1,0:T(8,128)(2,1)S(1)} %get-tuple-element.50, ...), kind=kOutput, calls=%fused_computation.46 | convolution fusion | flops 2165309440 | bytes 12582912 | tf_op jit(solution)/shard_map/dot_general | solution.py:392
  (177 shorter events, 56.4 us)
Async XLA Ops:
  14.4 27.0 %collective-permute-start.2 = (bf16[64,4096]{1,0:T(8,128)(2,1)S(1)}, bf16[64,4096]{1,0:T(8,128)(2,1)}, u32[]{:S(2)}, u32[]{:S(2)}) collective-permute-start(bf16[64,4096]{1,0:T(8,128)(2,1)S(1)} %bitcast_select_fusion), channel_id=1, source_target_pairs={{0,2},{2,0},{4,6},{6,4},{1,3},{3,1},{5,7},{7,5},{8,10},{10,8},{12,... | collective-permute-start | bytes 1572872 | tf_op jit(solution)/shard_map/ppermute | solution.py:238
  15.8 25.9 %collective-permute-start.1 = (bf16[64,4096]{1,0:T(8,128)(2,1)S(1)}, bf16[64,4096]{1,0:T(8,128)(2,1)}, u32[]{:S(2)}, u32[]{:S(2)}) collective-permute-start(bf16[64,4096]{1,0:T(8,128)(2,1)S(1)} %bitcast_select_fusion), channel_id=1, source_target_pairs={{0,1},{1,0},{2,3},{3,2},{4,5},{5,4},{6,7},{7,6},{8,9},{9,8},{10,11... | collective-permute-start | bytes 1572872 | tf_op jit(solution)/shard_map/ppermute | solution.py:238
  17.0 19.9 %collective-permute-start.4 = (bf16[64,4096]{1,0:T(8,128)(2,1)S(1)}, bf16[64,4096]{1,0:T(8,128)(2,1)}, u32[]{:S(2)}, u32[]{:S(2)}) collective-permute-start(bf16[64,4096]{1,0:T(8,128)(2,1)S(1)} %bitcast_select_fusion), channel_id=1, source_target_pairs={{0,4},{2,6},{4,0},{6,2},{1,5},{3,7},{5,1},{7,3},{8,12},{10,14},{12... | collective-permute-start | bytes 1572872 | tf_op jit(solution)/shard_map/ppermute | solution.py:238
  23.1 19.8 %collective-permute-start.10 = (bf16[4,128,1024]{2,1,0:T(8,128)(2,1)}, bf16[4,128,1024]{2,1,0:T(8,128)(2,1)}, u32[]{:S(2)}, u32[]{:S(2)}) collective-permute-start(bf16[4,128,1024]{2,1,0:T(8,128)(2,1)} %pad_maximum_fusion.4), channel_id=1, source_target_pairs={{0,8},{8,16},{16,24},{24,0},{1,9},{9,17},{17,25},{25,1},{2,10},{10... | collective-permute-start | bytes 3145736 | tf_op jit(solution)/shard_map/ppermute | solution.py:234
  37.0 34.5 %collective-permute-start.5 = (bf16[64,4096]{1,0:T(8,128)(2,1)}, bf16[64,4096]{1,0:T(8,128)(2,1)S(1)}, u32[]{:S(2)}, u32[]{:S(2)}) collective-permute-start(bf16[64,4096]{1,0:T(8,128)(2,1)} %collective-permute-done.4), channel_id=1, source_target_pairs={{0,1},{1,0},{2,3},{3,2},{4,5},{5,4},{6,7},{7,6},{8,9},{9,8},{10,11... | collective-permute-start | bytes 1572872 | tf_op jit(solution)/shard_map/ppermute | solution.py:238
  38.2 40.4 %collective-permute-start.6 = (bf16[64,4096]{1,0:T(8,128)(2,1)}, bf16[64,4096]{1,0:T(8,128)(2,1)S(1)}, u32[]{:S(2)}, u32[]{:S(2)}) collective-permute-start(bf16[64,4096]{1,0:T(8,128)(2,1)} %collective-permute-done.4), channel_id=1, source_target_pairs={{0,2},{2,0},{4,6},{6,4},{1,3},{3,1},{5,7},{7,5},{8,10},{10,8},{12,... | collective-permute-start | bytes 1572872 | tf_op jit(solution)/shard_map/ppermute | solution.py:238
  41.5 13.7 %collective-permute-start.3 = (bf16[64,4096]{1,0:T(8,128)(2,1)}, bf16[64,4096]{1,0:T(8,128)(2,1)S(1)}, u32[]{:S(2)}, u32[]{:S(2)}) collective-permute-start(bf16[64,4096]{1,0:T(8,128)(2,1)} %collective-permute-done.2), channel_id=1, source_target_pairs={{0,1},{1,0},{2,3},{3,2},{4,5},{5,4},{6,7},{7,6},{8,9},{9,8},{10,11... | collective-permute-start | bytes 1572872 | tf_op jit(solution)/shard_map/ppermute | solution.py:238
  44.5 50.5 %collective-permute-start.11 = (bf16[128,1024]{1,0:T(8,128)(2,1)S(1)}, bf16[128,1024]{1,0:T(8,128)(2,1)S(1)}, u32[]{:S(2)}, u32[]{:S(2)}) collective-permute-start(bf16[128,1024]{1,0:T(8,128)(2,1)S(1)} %get-tuple-element.68), channel_id=1, source_target_pairs={{0,2},{2,0},{4,6},{6,4},{1,3},{3,1},{5,7},{7,5},{8,10},{10,8},{12,... | collective-permute-start | bytes 786440 | tf_op jit(solution)/shard_map/ppermute | solution.py:238
  44.6 35.2 %collective-permute-start.16 = (bf16[64,1024]{1,0:T(8,128)(2,1)S(1)}, bf16[64,1024]{1,0:T(8,128)(2,1)S(1)}, u32[]{:S(2)}, u32[]{:S(2)}) collective-permute-start(bf16[64,1024]{1,0:T(8,128)(2,1)S(1)} %get-tuple-element.77), channel_id=1, source_target_pairs={{0,16},{8,24},{16,0},{24,8},{1,17},{9,25},{17,1},{25,9},{2,18},{10... | collective-permute-start | bytes 393224 | tf_op jit(solution)/shard_map/ppermute | solution.py:238
  55.2 27.5 %collective-permute-start.17 = (bf16[64,1024]{1,0:T(8,128)(2,1)S(1)}, bf16[64,1024]{1,0:T(8,128)(2,1)S(1)}, u32[]{:S(2)}, u32[]{:S(2)}) collective-permute-start(bf16[64,1024]{1,0:T(8,128)(2,1)S(1)} %get-tuple-element.78), channel_id=1, source_target_pairs={{0,24},{8,16},{16,8},{24,0},{1,25},{9,17},{17,9},{25,1},{2,26},{10... | collective-permute-start | bytes 393224 | tf_op jit(solution)/shard_map/ppermute | solution.py:238
  73.2 9.5 %collective-permute-start.13 = (bf16[128,1024]{1,0:T(8,128)(2,1)S(1)}, bf16[128,1024]{1,0:T(8,128)(2,1)S(1)}, u32[]{:S(2)}, u32[]{:S(2)}) collective-permute-start(bf16[128,1024]{1,0:T(8,128)(2,1)S(1)} %get-tuple-element.66), channel_id=1, source_target_pairs={{0,6},{2,4},{4,2},{6,0},{1,7},{3,5},{5,3},{7,1},{8,14},{10,12},{12... | collective-permute-start | bytes 786440 | tf_op jit(solution)/shard_map/ppermute | solution.py:238
  78.6 27.2 %collective-permute-start.12 = (bf16[128,1024]{1,0:T(8,128)(2,1)S(1)}, bf16[128,1024]{1,0:T(8,128)(2,1)S(1)}, u32[]{:S(2)}, u32[]{:S(2)}) collective-permute-start(bf16[128,1024]{1,0:T(8,128)(2,1)S(1)} %get-tuple-element.67), channel_id=1, source_target_pairs={{0,4},{2,6},{4,0},{6,2},{1,5},{3,7},{5,1},{7,3},{8,12},{10,14},{12... | collective-permute-start | bytes 786440 | tf_op jit(solution)/shard_map/ppermute | solution.py:238
  79.8 50.9 %collective-permute-start.8 = (bf16[256,1024]{1,0:T(8,128)(2,1)}, bf16[256,1024]{1,0:T(8,128)(2,1)}, u32[]{:S(2)}, u32[]{:S(2)}) collective-permute-start(bf16[256,1024]{1,0:T(8,128)(2,1)} %get-tuple-element.48), channel_id=1, source_target_pairs={{0,8},{8,0},{16,24},{24,16},{1,9},{9,1},{17,25},{25,17},{2,10},{10... | collective-permute-start | bytes 1572872 | tf_op jit(solution)/shard_map/ppermute | solution.py:238
  82.7 26.0 %collective-permute-start.7 = (bf16[64,4096]{1,0:T(8,128)(2,1)S(1)}, bf16[64,4096]{1,0:T(8,128)(2,1)S(1)}, u32[]{:S(2)}, u32[]{:S(2)}) collective-permute-start(bf16[64,4096]{1,0:T(8,128)(2,1)S(1)} %collective-permute-done.6), channel_id=1, source_target_pairs={{0,1},{1,0},{2,3},{3,2},{4,5},{5,4},{6,7},{7,6},{8,9},{9,8},{10,11... | collective-permute-start | bytes 1572872 | tf_op jit(solution)/shard_map/ppermute | solution.py:238
  82.7 44.3 %collective-permute-start.19 = (bf16[2,64,1024]{2,1,0:T(8,128)(2,1)S(1)}, bf16[2,64,1024]{2,1,0:T(8,128)(2,1)}, u32[]{:S(2)}, u32[]{:S(2)}) collective-permute-start(bf16[2,64,1024]{2,1,0:T(8,128)(2,1)S(1)} %pad_maximum_fusion.13), channel_id=1, source_target_pairs={{0,4},{2,6},{4,0},{6,2},{1,5},{3,7},{5,1},{7,3},{8,12},{10,14},{12... | collective-permute-start | bytes 786440 | tf_op jit(solution)/shard_map/ppermute | solution.py:238
  94.9 34.9 %collective-permute-start.18 = (bf16[2,64,1024]{2,1,0:T(8,128)(2,1)S(1)}, bf16[2,64,1024]{2,1,0:T(8,128)(2,1)}, u32[]{:S(2)}, u32[]{:S(2)}) collective-permute-start(bf16[2,64,1024]{2,1,0:T(8,128)(2,1)S(1)} %pad_maximum_fusion.13), channel_id=1, source_target_pairs={{0,2},{2,0},{4,6},{6,4},{1,3},{3,1},{5,7},{7,5},{8,10},{10,8},{12,... | collective-permute-start | bytes 786440 | tf_op jit(solution)/shard_map/ppermute | solution.py:238
  105.8 43.4 %collective-permute-start.14 = (bf16[2,256,1024]{2,1,0:T(8,128)(2,1)S(1)}, bf16[2,256,1024]{2,1,0:T(8,128)(2,1)}, u32[]{:S(2)}, u32[]{:S(2)}) collective-permute-start(bf16[2,256,1024]{2,1,0:T(8,128)(2,1)S(1)} %bitcast.140), channel_id=1, source_target_pairs={{0,8},{8,0},{16,24},{24,16},{1,9},{9,1},{17,25},{25,17},{2,10},{10... | collective-permute-start | bytes 3145736 | tf_op jit(solution)/shard_map/ppermute | solution.py:238
  108.7 38.6 %collective-permute-start.22 = (bf16[2,256,1024]{2,1,0:T(8,128)(2,1)S(1)}, bf16[2,256,1024]{2,1,0:T(8,128)(2,1)}, u32[]{:S(2)}, u32[]{:S(2)}) collective-permute-start(bf16[2,256,1024]{2,1,0:T(8,128)(2,1)S(1)} %bitcast.141), channel_id=1, source_target_pairs={{0,16},{8,24},{16,0},{24,8},{1,17},{9,25},{17,1},{25,9},{2,18},{10... | collective-permute-start | bytes 3145736 | tf_op jit(solution)/shard_map/ppermute | solution.py:238
  131.6 13.6 %collective-permute-start.9 = (bf16[256,1024]{1,0:T(8,128)(2,1)S(1)}, bf16[256,1024]{1,0:T(8,128)(2,1)}, u32[]{:S(2)}, u32[]{:S(2)}) collective-permute-start(bf16[256,1024]{1,0:T(8,128)(2,1)S(1)} %get-tuple-element.47), channel_id=1, source_target_pairs={{0,8},{8,0},{16,24},{24,16},{1,9},{9,1},{17,25},{25,17},{2,10},{10... | collective-permute-start | bytes 1572872 | tf_op jit(solution)/shard_map/ppermute | solution.py:238
  136.6 23.3 %collective-permute-start.23 = (bf16[2,256,1024]{2,1,0:T(8,128)(2,1)S(1)}, bf16[2,256,1024]{2,1,0:T(8,128)(2,1)}, u32[]{:S(2)}, u32[]{:S(2)}) collective-permute-start(bf16[2,256,1024]{2,1,0:T(8,128)(2,1)S(1)} %bitcast.142), channel_id=1, source_target_pairs={{0,16},{8,24},{16,0},{24,8},{1,17},{9,25},{17,1},{25,9},{2,18},{10... | collective-permute-start | bytes 3145736 | tf_op jit(solution)/shard_map/ppermute | solution.py:238
  142.4 21.2 %collective-permute-start.15 = (bf16[2,256,1024]{2,1,0:T(8,128)(2,1)S(1)}, bf16[2,256,1024]{2,1,0:T(8,128)(2,1)S(1)}, u32[]{:S(2)}, u32[]{:S(2)}) collective-permute-start(bf16[2,256,1024]{2,1,0:T(8,128)(2,1)S(1)} %bitcast.143), channel_id=1, source_target_pairs={{0,8},{8,0},{16,24},{24,16},{1,9},{9,1},{17,25},{25,17},{2,10},{10... | collective-permute-start | bytes 3145736 | tf_op jit(solution)/shard_map/ppermute | solution.py:238
  145.3 25.9 %collective-permute-start.21 = (bf16[4,2,64,1024]{3,2,1,0:T(8,128)(2,1)S(1)}, bf16[4,2,64,1024]{3,2,1,0:T(8,128)(2,1)S(1)}, u32[]{:S(2)}, u32[]{:S(2)}) collective-permute-start(bf16[4,2,64,1024]{3,2,1,0:T(8,128)(2,1)S(1)} %pad_maximum_fusion.5), channel_id=1, source_target_pairs={{0,1},{1,0},{2,3},{3,2},{4,5},{5,4},{6,7},{7,6},{8,9},{9,8},{10,11... | collective-permute-start | bytes 3145736 | tf_op jit(solution)/shard_map/ppermute | solution.py:238
  147.3 27.6 %collective-permute-start.24 = (bf16[2,256,1024]{2,1,0:T(8,128)(2,1)}, bf16[2,256,1024]{2,1,0:T(8,128)(2,1)S(1)}, u32[]{:S(2)}, u32[]{:S(2)}) collective-permute-start(bf16[2,256,1024]{2,1,0:T(8,128)(2,1)} %collective-permute-done.22), channel_id=1, source_target_pairs={{0,8},{8,0},{16,24},{24,16},{1,9},{9,1},{17,25},{25,17},{2,10},{10... | collective-permute-start | bytes 3145736 | tf_op jit(solution)/shard_map/ppermute | solution.py:238
  159.9 15.1 %collective-permute-start.25 = (bf16[2,256,1024]{2,1,0:T(8,128)(2,1)}, bf16[2,256,1024]{2,1,0:T(8,128)(2,1)S(1)}, u32[]{:S(2)}, u32[]{:S(2)}) collective-permute-start(bf16[2,256,1024]{2,1,0:T(8,128)(2,1)} %collective-permute-done.23), channel_id=1, source_target_pairs={{0,8},{8,0},{16,24},{24,16},{1,9},{9,1},{17,25},{25,17},{2,10},{10... | collective-permute-start | bytes 3145736 | tf_op jit(solution)/shard_map/ppermute | solution.py:238
  (29 other events, 380.6 us)
where the time goes:
time: 185 us; the launch traced here: 184 us
  starting transfers between devices  53.7 us (29%)
  waiting for transfers between devices  39 us (21%)
  matrix products  33.3 us (18%)
  local copies, waits for them, and re-layouts  25.3 us (14%)
  Pallas kernels  19 us (10%)
  other arithmetic  10.7 us (6%)
  between operations  3.32 us (2%)
    ppermute x27, starting transfers between devices, swapped(): return lax.ppermute(shard, axis, xor_pairs(lax.axis_size(axis), by))  47.7 us
    ppermute x27, waiting for transfers between devices, swapped(): return lax.ppermute(shard, axis, xor_pairs(lax.axis_size(axis), by))  37.1 us
    pallas_call x2, Pallas kernels, scan_backward(): pl.pallas_call(scan_kernel, grid=(groups, blocks), in_specs=[pl.BlockSpec...  19 us
    dot_general x4, matrix products, product(): lax.dot_general(x_all, g_all, (((0,), (0,)), ((), ())), preferred_element...  16.4 us
    unnamed x56, local copies, waits for them, and re-layouts  9.64 us
    dot_general x2, matrix products, per_device(): jnp.dot(xs, w_x, preferred_element_type=F32)  8.17 us
    ppermute x2, starting transfers between devices, shifted(): lax.ppermute(shard, axis, [(i, (i + by) % size) for i in range(size)])  6 us
    select_n x5, other arithmetic, in_order(): first = jnp.where(member == 0, mine, other)  4.85 us
  transfers between devices with their start and end apart: 29, of which 7 were waited for; matrix products, arithmetic and copies ran while one was open for 30% of the time, Pallas kernels for 10%

commit v1 on v0

--- a/solution.py
+++ b/solution.py
@@ -7,7 +7,7 @@
 
 NORM_GROUP = 512
 PAIR = 128
-CHUNKS = 2
+CUTS = (2, 4)
 F32 = jnp.float32
 BF16 = jnp.bfloat16
 
@@ -300,8 +300,12 @@
         return lax.dynamic_slice(tokens, (slot, member * half, zero), (1, half, width))[0]
 
     mine_x = jnp.where(came, shifted(half_rows(own_send), "dp", 1), half_rows(zero))
-    mine = across(mine_x)
-    x_blocks = [in_order(part, swapped(part, "tensor", 1)) for part in mine]
+    mine = [mine_x]
+    for k in range(1, fsdp_count):
+        low = k & -k
+        mine.append(swapped(after(mine[k ^ low], mine[low // 2]), "fsdp", low))
+    other = [swapped(part, "tensor", 1) for part in mine]
+    x_blocks = [in_order(part, rest) for part, rest in zip(mine, other, strict=True)]
 
     held_d = after(cotangent, mine_x)
 
@@ -317,16 +321,15 @@
     d_blocks = []
     for k in range(fsdp_count):
         part = lax.dynamic_index_in_dim(mine_d, column ^ k, 0, keepdims=False)
+        part = after(part, mine[k]) if k > 1 else part
         d_blocks.append(swapped(part, "fsdp", k) if k else part)
 
     def columns_for(rows, m):
         at = (zero,) * (rows.ndim - 1) + ((dp_index ^ m) * piece,)
         return lax.dynamic_slice(rows, at, rows.shape[:-1] + (piece,))
 
-    held_x = after(mine_x, mine_d)
-    far_x = jnp.stack([swapped(columns_for(held_x, m), "dp", m) for m in range(2, dp_count)])
-    far_x = after(far_x, d_blocks[-1], mine[-1])
-    far_x = jnp.stack(across(far_x))
+    far_x = jnp.stack([swapped(columns_for(mine_x, m), "dp", m) for m in range(2, dp_count)])
+    far_x = jnp.stack(across(after(far_x, other[-1], d_blocks[-1])))
     far_x = in_order(far_x, swapped(far_x, "tensor", 1))
 
     columns = column ^ jnp.arange(fsdp_count, dtype=jnp.int32)
@@ -342,14 +345,15 @@
     ends = jnp.stack(ends, axis=1)
     skip_chan = jnp.repeat(skip_scale, chan // head_count)
 
-    per_chunk = max(1, fsdp_count // CHUNKS)
+    cuts = [0] + [fsdp_count * part // 4 for part in CUTS]
     x_parts = [[] for _ in range(dp_count)]
     g_parts = [[] for _ in range(dp_count)]
     dt_parts = []
+    partner_cols = []
     channel_parts = []
     head_parts = []
-    for first in range(0, fsdp_count, per_chunk):
-        last = first + per_chunk
+    for first, last in zip(cuts, cuts[1:]):
+        per_chunk = last - first
         xs = jnp.concatenate(x_blocks[first:last], axis=0)
         cot = jnp.stack(d_blocks[first:last])
         px = jnp.dot(xs, w_x, preferred_element_type=F32).reshape(per_chunk, length, chan)
@@ -358,20 +362,22 @@
         bc = bc.reshape(per_chunk, length, w_bc.shape[1])
         pdt = lax.dot_general(w_dt, xs, (((0,), (1,)), ((), ())), preferred_element_type=F32)
         pdt = pdt.reshape(groups, head_count // groups, per_chunk, length).transpose(0, 2, 1, 3)
+        x_parts[0].append(columns_for(xs, 0))
+        partner_cols.append(columns_for(xs, 1))
+        if last == fsdp_count:
+            x_parts[1].append(swapped(jnp.concatenate(partner_cols, axis=0), "dp", 1))
+        due = [g_parts[1][-1]] if first else []
         gpre, gpdt, gch, gh = scan_backward(
             ends[first:last], px, pz, pdt, cot, bc,
-            conv_w, conv_b, norm_gain, skip_chan, a_log, dt_bias,
+            conv_w, conv_b, norm_gain, after(skip_chan, *due), a_log, dt_bias,
         )
         dt_parts.append(gpdt.transpose(1, 0, 2, 3).reshape(per_chunk, head_count, length))
         channel_parts.append(gch)
         head_parts.append(gh)
         gpre = gpre.reshape(2, per_chunk * length, chan)
         for m in range(0, dp_count, 2):
-            got = swapped(gpre, "dp", m) if m else gpre
-            g_parts[m].append(got)
-            g_parts[m + 1].append(swapped(got, "dp", 1))
-        x_parts[0].append(columns_for(xs, 0))
-        x_parts[1].append(swapped(columns_for(xs, 1), "dp", 1))
+            g_parts[m].append(swapped(gpre, "dp", m) if m else gpre)
+            g_parts[m + 1].append(swapped(g_parts[m][-1], "dp", 1))
         for m in range(2, dp_count):
             x_parts[m].append(far_x[first:last, m - 2].reshape(-1, piece))
 
@@ -380,24 +386,25 @@
     heads = sum(head_parts[1:], head_parts[0]).reshape(head_count, 3).T
     rows.append(jnp.pad(heads.reshape(1, -1), ((0, 0), (0, chan - 3 * head_count))))
     packed = jnp.concatenate(rows, axis=0)
-    packs = [packed if m == 0 else swapped(packed, "dp", m) for m in range(dp_count)]
+    packed = after(packed, g_parts[1][-1])
+    packs = jnp.stack([packed] + [swapped(packed, "dp", m) for m in range(2, dp_count, 2)])
+    packs = jnp.stack((packs, swapped(packs, "dp", 1)), axis=1).reshape((dp_count,) + packed.shape)
     dt_rows = gpdt.shape[0]
-    small = tree_sum([p[dt_rows:] for p in packs])
+    small = tree_sum([packs[m, dt_rows:] for m in range(dp_count)])
     channel_sum = small[: taps + 2]
     head_sum = small[taps + 2, : 3 * head_count].reshape(3, head_count)
 
+    dt_all = packs[:, :dt_rows].reshape(dp_count * fsdp_count, head_count, length)
+    dt_all = dt_all.astype(BF16).transpose(1, 0, 2).reshape(head_count, -1)
     def product(ms, which):
         x_all = jnp.concatenate([p for m in ms for p in x_parts[m]], axis=0)
         g_all = jnp.concatenate([p[which] for m in ms for p in g_parts[m]], axis=0)
         return lax.dot_general(x_all, g_all, (((0,), (0,)), ((), ())), preferred_element_type=F32)
 
-    near = tuple(range(2))
-    far = tuple(range(2, dp_count))
+    near, far = tuple(range(2)), tuple(range(2, dp_count))
     grad_x = product(near, 0) + product(far, 0)
     grad_z = product(near, 1) + product(far, 1)
     x_all = jnp.concatenate([p for parts in x_parts for p in parts], axis=0)
-    dt_all = jnp.concatenate([p[:dt_rows].reshape(-1, head_count, length) for p in packs], axis=0)
-    dt_all = dt_all.astype(BF16).transpose(1, 0, 2).reshape(head_count, -1)
     grad_dt = lax.dot_general(x_all, dt_all, (((0,), (1,)), ((), ())), preferred_element_type=F32)
     return grad_x, grad_z, grad_dt, channel_sum, head_sum
 

time: 185 us -> 168 us (0.908)
  starting transfers between devices: 53.7 us -> 30.6 us
  local copies, waits for them, and re-layouts: 25.3 us -> 30.1 us
  waiting for transfers between devices: 39 us -> 42.9 us
  other arithmetic: 10.7 us -> 7.6 us
    ppermute x27 -> x25, starting transfers between devices: 47.7 us -> 27.9 us  [swapped(): return lax.ppermute(shard, axis, xor_pairs(lax.axis_size(axis), by))]
    squeeze x6, local copies, waits for them, and re-layouts: 4.19 us -> 8.21 us  [product(): g_all = jnp.concatenate([p[which] for m in ms for p in g_parts[m]], axis=0)]
    dot_general x4, matrix products: 16.4 us -> 20.4 us  [product(): lax.dot_general(x_all, g_all, (((0,), (0,)), ((), ())), preferred_element...]
    ppermute x2, waiting for transfers between devices: 1.9 us -> 5.52 us  [shifted(): lax.ppermute(shard, axis, [(i, (i + by) % size) for i in range(size)])]
    dot_general x2, matrix products: 8.17 us -> 4.82 us  [per_device(): jnp.dot(xs, w_x, preferred_element_type=F32)]
    ppermute x2, starting transfers between devices: 6 us -> 2.74 us  [shifted(): lax.ppermute(shard, axis, [(i, (i + by) % size) for i in range(size)])]
    select_n x5, other arithmetic: 4.85 us -> 1.63 us  [in_order(): first = jnp.where(member == 0, mine, other)]
    unnamed x56 -> x53, local copies, waits for them, and re-layouts: 9.64 us -> 8.52 us
  transfers between devices with their start and end apart: 29 -> 27, of which waited for: 7 -> 12; matrix products, arithmetic and copies ran while one was open for 30% -> 33% of each run, Pallas kernels for 10% -> 11%
where the time goes in v1:
time: 168 us; the launch traced here: 167 us
  waiting for transfers between devices  42.9 us (26%)
  matrix products  34 us (20%)
  starting transfers between devices  30.6 us (18%)
  local copies, waits for them, and re-layouts  30.1 us (18%)
  Pallas kernels  19 us (11%)
  other arithmetic  7.6 us (5%)
  between operations  3.31 us (2%)
    ppermute x25, waiting for transfers between devices, swapped(): return lax.ppermute(shard, axis, xor_pairs(lax.axis_size(axis), by))  37.3 us
    ppermute x25, starting transfers between devices, swapped(): return lax.ppermute(shard, axis, xor_pairs(lax.axis_size(axis), by))  27.9 us
    dot_general x4, matrix products, product(): lax.dot_general(x_all, g_all, (((0,), (0,)), ((), ())), preferred_element...  20.4 us
    pallas_call x2, Pallas kernels, scan_backward(): pl.pallas_call(scan_kernel, grid=(groups, blocks), in_specs=[pl.BlockSpec...  19 us
    unnamed x53, local copies, waits for them, and re-layouts  8.52 us
    squeeze x6, local copies, waits for them, and re-layouts, product(): g_all = jnp.concatenate([p[which] for m in ms for p in g_parts[m]], axis=0)  8.21 us
    ppermute x2, waiting for transfers between devices, shifted(): lax.ppermute(shard, axis, [(i, (i + by) % size) for i in range(size)])  5.52 us
    dot_general x2, matrix products, per_device(): jnp.dot(xs, w_x, preferred_element_type=F32)  4.82 us
  transfers between devices with their start and end apart: 27, of which 12 were waited for; matrix products, arithmetic and copies ran while one was open for 33% of the time, Pallas kernels for 11%

profile of v1, /device:TPU:1, one launch (start us, length us, event | category | flops | bytes accessed | tf_op | source)
XLA Modules:
  0.0 167.5 jit_solution(10371408938650711773)
XLA Ops:
  4.5 2.7 %collective-permute-start = (bf16[64,4096]{1,0:T(8,128)(2,1)S(1)}, bf16[64,4096]{1,0:T(8,128)(2,1)S(1)}, u32[]{:S(2)}, u32[]{:S(2)}) collective-permute-start(bf16[64,4096]{1,0:T(8,128)(2,1)S(1)} %dynamic-slice_bitcast_fusion), channel_id=1, source_target_pairs={{0,8},{8,16},{16,24},{24,0},{1,9},{9,17},{17,25},{25,1},{2,10},{10... | collective-permute-start | bytes 1572872 | tf_op jit(solution)/shard_map/ppermute | solution.py:234
  17.8 2.8 %collective-permute-start.16 = (bf16[64,1024]{1,0:T(8,128)(2,1)S(1)}, bf16[64,1024]{1,0:T(8,128)(2,1)S(1)}, u32[]{:S(2)}, u32[]{:S(2)}) collective-permute-start(bf16[64,1024]{1,0:T(8,128)(2,1)S(1)} %get-tuple-element.88), channel_id=1, source_target_pairs={{0,24},{8,16},{16,8},{24,0},{1,25},{9,17},{17,9},{25,1},{2,26},{10... | collective-permute-start | bytes 393224 | tf_op jit(solution)/shard_map/ppermute | solution.py:238
  22.9 4.0 %collective-permute-done.16 = bf16[64,1024]{1,0:T(8,128)(2,1)S(1)} collective-permute-done((bf16[64,1024]{1,0:T(8,128)(2,1)S(1)}, bf16[64,1024]{1,0:T(8,128)(2,1)S(1)}, u32[]{:S(2)}, u32[]{:S(2)}) %collective-permute-start.16) | collective-permute-done | bytes 131104 | tf_op jit(solution)/shard_map/ppermute | solution.py:238
  28.4 2.3 %collective-permute-start.4 = (bf16[64,4096]{1,0:T(8,128)(2,1)S(1)}, bf16[64,4096]{1,0:T(8,128)(2,1)S(1)}, u32[]{:S(2)}, u32[]{:S(2)}) collective-permute-start(bf16[64,4096]{1,0:T(8,128)(2,1)S(1)} %bitcast_select_fusion), channel_id=1, source_target_pairs={{0,4},{2,6},{4,0},{6,2},{1,5},{3,7},{5,1},{7,3},{8,12},{10,14},{12... | collective-permute-start | bytes 1572872 | tf_op jit(solution)/shard_map/ppermute | solution.py:238
  31.1 5.5 %collective-permute-done.9 = bf16[4,128,1024]{2,1,0:T(8,128)(2,1)S(1)} collective-permute-done((bf16[4,128,1024]{2,1,0:T(8,128)(2,1)S(1)}, bf16[4,128,1024]{2,1,0:T(8,128)(2,1)S(1)}, u32[]{:S(2)}, u32[]{:S(2)}) %collective-permute-start.9) | collective-permute-done | bytes 1048608 | tf_op jit(solution)/shard_map/ppermute | solution.py:234
  37.1 4.7 %collective-permute-done.3 = bf16[64,4096]{1,0:T(8,128)(2,1)S(1)} collective-permute-done((bf16[64,4096]{1,0:T(8,128)(2,1)S(1)}, bf16[64,4096]{1,0:T(8,128)(2,1)S(1)}, u32[]{:S(2)}, u32[]{:S(2)}) %collective-permute-start.3) | collective-permute-done | bytes 524320 | tf_op jit(solution)/shard_map/ppermute | solution.py:238
  42.2 2.4 %fusion.57 = f32[256,1024]{1,0:T(8,128)S(1)} fusion(bf16[256,4096]{1,0:T(8,128)(2,1)S(1)} %pad_maximum_fusion, bf16[4096,1024]{1,0:T(8,128)(2,1)S(1)} %bitcast.200), kind=kOutput, calls=%fused_computation.152 | convolution fusion | flops 2147483648 | bytes 11534336 | tf_op jit(solution)/shard_map/dot_general | solution.py:359
  45.4 2.4 %fusion.58 = f32[256,1024]{1,0:T(8,128)S(1)} fusion(bf16[256,4096]{1,0:T(8,128)(2,1)S(1)} %pad_maximum_fusion, bf16[4096,1024]{1,0:T(8,128)(2,1)S(1)} %bitcast.202), kind=kOutput, calls=%fused_computation.153 | convolution fusion | flops 2147483648 | bytes 11534336 | tf_op jit(solution)/shard_map/dot_general | solution.py:360
  49.4 4.0 %collective-permute-done.4 = bf16[64,4096]{1,0:T(8,128)(2,1)S(1)} collective-permute-done((bf16[64,4096]{1,0:T(8,128)(2,1)S(1)}, bf16[64,4096]{1,0:T(8,128)(2,1)S(1)}, u32[]{:S(2)}, u32[]{:S(2)}) %collective-permute-start.4) | collective-permute-done | bytes 524320 | tf_op jit(solution)/shard_map/ppermute | solution.py:238
  53.4 4.6 %collective-permute-start.6 = (bf16[64,4096]{1,0:T(8,128)(2,1)S(1)}, bf16[64,4096]{1,0:T(8,128)(2,1)S(1)}, u32[]{:S(2)}, u32[]{:S(2)}) collective-permute-start(bf16[64,4096]{1,0:T(8,128)(2,1)S(1)} %collective-permute-done.4), channel_id=1, source_target_pairs={{0,2},{2,0},{4,6},{6,4},{1,3},{3,1},{5,7},{7,5},{8,10},{10,8},{12,... | collective-permute-start | bytes 1572872 | tf_op jit(solution)/shard_map/ppermute | solution.py:238
  59.4 9.5 %shard_map.173 = (bf16[2,2,128,1024]{3,2,1,0:T(8,128)(2,1)S(1)}, f32[2,2,8,128]{3,2,1,0:T(8,128)S(1)}, f32[6,1024]{1,0:T(8,128)S(1)}, f32[2,8,3]{2,1,0:T(8,128)S(1)}) custom-call(s32[2,3]{1,0:T(2,128)S(1)} %get-tuple-element.91.ends_ref, f32[2,128,1024]{2,1,0:T(8,128)S(1)} %bitcast.155, f32[2,128,1024]{2,1,0:T(8,128)S(1)} %bitcast.156, ...), custom_call_target="tpu_custom_call" | custom-call | flops 104857600 | bytes 4718592 | tf_op jit(solution)/shard_map/pallas_call | solution.py:192
  73.0 3.3 %collective-permute-start.12 = (bf16[128,1024]{1,0:T(8,128)(2,1)S(1)}, bf16[128,1024]{1,0:T(8,128)(2,1)S(1)}, u32[]{:S(2)}, u32[]{:S(2)}) collective-permute-start(bf16[128,1024]{1,0:T(8,128)(2,1)S(1)} %get-tuple-element.28), channel_id=1, source_target_pairs={{0,6},{2,4},{4,2},{6,0},{1,7},{3,5},{5,3},{7,1},{8,14},{10,12},{12... | collective-permute-start | bytes 786440 | tf_op jit(solution)/shard_map/ppermute | solution.py:238
  76.7 4.7 %collective-permute-done.12 = bf16[128,1024]{1,0:T(8,128)(2,1)S(1)} collective-permute-done((bf16[128,1024]{1,0:T(8,128)(2,1)S(1)}, bf16[128,1024]{1,0:T(8,128)(2,1)S(1)}, u32[]{:S(2)}, u32[]{:S(2)}) %collective-permute-start.12) | collective-permute-done | bytes 262176 | tf_op jit(solution)/shard_map/ppermute | solution.py:238
  81.5 6.8 %collective-permute-done.7 = bf16[64,4096]{1,0:T(8,128)(2,1)S(1)} collective-permute-done((bf16[64,4096]{1,0:T(8,128)(2,1)S(1)}, bf16[64,4096]{1,0:T(8,128)(2,1)S(1)}, u32[]{:S(2)}, u32[]{:S(2)}) %collective-permute-start.7) | collective-permute-done | bytes 524320 | tf_op jit(solution)/shard_map/ppermute | solution.py:238
  88.6 2.4 %fusion.59 = f32[256,1024]{1,0:T(8,128)S(1)} fusion(bf16[256,4096]{1,0:T(8,128)(2,1)S(1)} %pad_maximum_fusion.1, bf16[4096,1024]{1,0:T(8,128)(2,1)S(1)} %bitcast.200), kind=kOutput, calls=%fused_computation.154 | convolution fusion | flops 2147483648 | bytes 11534336 | tf_op jit(solution)/shard_map/dot_general | solution.py:359
  93.9 2.4 %collective-permute-start.8 = (bf16[512,1024]{1,0:T(8,128)(2,1)}, bf16[512,1024]{1,0:T(8,128)(2,1)}, u32[]{:S(2)}, u32[]{:S(2)}) collective-permute-start(bf16[512,1024]{1,0:T(8,128)(2,1)} %pad_maximum_fusion.4), channel_id=1, source_target_pairs={{0,8},{8,0},{16,24},{24,16},{1,9},{9,1},{17,25},{25,17},{2,10},{10... | collective-permute-start | bytes 3145736 | tf_op jit(solution)/shard_map/ppermute | solution.py:238
  97.0 2.4 %fusion.60 = f32[256,1024]{1,0:T(8,128)S(1)} fusion(bf16[256,4096]{1,0:T(8,128)(2,1)S(1)} %pad_maximum_fusion.1, bf16[4096,1024]{1,0:T(8,128)(2,1)S(1)} %bitcast.202), kind=kOutput, calls=%fused_computation.155 | convolution fusion | flops 2147483648 | bytes 11534336 | tf_op jit(solution)/shard_map/dot_general | solution.py:360
  99.4 9.5 %shard_map.174 = (bf16[2,2,128,1024]{3,2,1,0:T(8,128)(2,1)S(1)}, f32[2,2,8,128]{3,2,1,0:T(8,128)S(1)}, f32[6,1024]{1,0:T(8,128)S(1)}, f32[2,8,3]{2,1,0:T(8,128)S(1)}) custom-call(s32[2,3]{1,0:T(2,128)S(1)} %get-tuple-element.92.ends_ref, f32[2,128,1024]{2,1,0:T(8,128)S(1)} %bitcast.157, f32[2,128,1024]{2,1,0:T(8,128)S(1)} %bitcast.158, ...), custom_call_target="tpu_custom_call" | custom-call | flops 104857600 | bytes 4718592 | tf_op jit(solution)/shard_map/pallas_call | solution.py:192
  114.5 3.9 %collective-permute-done.17 = bf16[2,64,1024]{2,1,0:T(8,128)(2,1)S(1)} collective-permute-done((bf16[2,64,1024]{2,1,0:T(8,128)(2,1)S(1)}, bf16[2,64,1024]{2,1,0:T(8,128)(2,1)S(1)}, u32[]{:S(2)}, u32[]{:S(2)}) %collective-permute-start.17) | collective-permute-done | bytes 262176 | tf_op jit(solution)/shard_map/ppermute | solution.py:238
  120.3 3.6 %collective-permute-done.19 = bf16[2,64,1024]{2,1,0:T(8,128)(2,1)S(1)} collective-permute-done((bf16[2,64,1024]{2,1,0:T(8,128)(2,1)}, bf16[2,64,1024]{2,1,0:T(8,128)(2,1)S(1)}, u32[]{:S(2)}, u32[]{:S(2)}) %collective-permute-start.19) | collective-permute-done | bytes 262176 | tf_op jit(solution)/shard_map/ppermute | solution.py:238
  135.5 5.7 %fusion.16 = f32[1024,1024]{1,0:T(8,128)} fusion(bf16[256,1024]{1,0:T(8,128)(2,1)S(1)} %get-tuple-element.73, bf16[256,1024]{1,0:T(8,128)(2,1)S(1)} %get-tuple-element.71, bf16[256,1024]{1,0:T(8,128)(2,1)S(1)} %bitcast.188, bf16[256,1024]{1,0:T(8,128)(2,1)S(1)} %bitcast.186, bf16[512,1024]{1,0:T(8,128)(2,1)} %collective-permute-done.8, ...), kind=kOutput, calls=%fused_computation.29 | convolution fusion | flops 2162163712 | bytes 8388608 | tf_op jit(solution)/shard_map/dot_general | solution.py:402
  141.1 5.6 %fusion = f32[1024,1024]{1,0:T(8,128)} fusion(bf16[256,1024]{1,0:T(8,128)(2,1)S(1)} %get-tuple-element.74, bf16[256,1024]{1,0:T(8,128)(2,1)S(1)} %get-tuple-element.72, bf16[256,1024]{1,0:T(8,128)(2,1)S(1)} %bitcast.187, bf16[256,1024]{1,0:T(8,128)(2,1)S(1)} %bitcast.185, bf16[512,1024]{1,0:T(8,128)(2,1)} %collective-permute-done.8, ...), kind=kOutput, calls=%fused_computation.12 | convolution fusion | flops 2162163712 | bytes 8388608 | tf_op jit(solution)/shard_map/dot_general | solution.py:402
  158.3 4.6 %fusion.32 = f32[1024,1024]{1,0:T(8,128)} fusion(f32[1024,1024]{1,0:T(8,128)S(1)} %copy-done.18, bf16[256,1024]{1,0:T(8,128)(2,1)S(1)} %get-tuple-element.65, bf16[256,1024]{1,0:T(8,128)(2,1)S(1)} %copy-done.16, bf16[256,1024]{1,0:T(8,128)(2,1)S(1)} %copy-done.14, bf16[256,1024]{1,0:T(8,128)(2,1)S(1)} %copy-done.12, bf16[256,1024]{1,0:T(8,128)(2,1)S(1)} %bitcast.177, ...), kind=kOutput, calls=%fused_computation.45 | convolution fusion | flops 2165309440 | bytes 12582912 | tf_op jit(solution)/shard_map/dot_general | solution.py:402
  162.9 4.5 %fusion.35 = f32[1024,1024]{1,0:T(8,128)} fusion(f32[1024,1024]{1,0:T(8,128)S(1)} %copy-done.17, bf16[256,1024]{1,0:T(8,128)(2,1)S(1)} %get-tuple-element.66, bf16[256,1024]{1,0:T(8,128)(2,1)S(1)} %copy-done.15, bf16[256,1024]{1,0:T(8,128)(2,1)S(1)} %copy-done.13, bf16[256,1024]{1,0:T(8,128)(2,1)S(1)} %copy-done.11, bf16[256,1024]{1,0:T(8,128)(2,1)S(1)} %bitcast.178, ...), kind=kOutput, calls=%fused_computation.46 | convolution fusion | flops 2165309440 | bytes 12582912 | tf_op jit(solution)/shard_map/dot_general | solution.py:402
  (166 shorter events, 59.7 us)
Async XLA Ops:
  4.5 9.3 %collective-permute-start = (bf16[64,4096]{1,0:T(8,128)(2,1)S(1)}, bf16[64,4096]{1,0:T(8,128)(2,1)S(1)}, u32[]{:S(2)}, u32[]{:S(2)}) collective-permute-start(bf16[64,4096]{1,0:T(8,128)(2,1)S(1)} %dynamic-slice_bitcast_fusion), channel_id=1, source_target_pairs={{0,8},{8,16},{16,24},{24,0},{1,9},{9,17},{17,25},{25,1},{2,10},{10... | collective-permute-start | bytes 1572872 | tf_op jit(solution)/shard_map/ppermute | solution.py:234
  14.9 16.1 %collective-permute-start.1 = (bf16[64,4096]{1,0:T(8,128)(2,1)S(1)}, bf16[64,4096]{1,0:T(8,128)(2,1)S(1)}, u32[]{:S(2)}, u32[]{:S(2)}) collective-permute-start(bf16[64,4096]{1,0:T(8,128)(2,1)S(1)} %bitcast_select_fusion), channel_id=1, source_target_pairs={{0,1},{1,0},{2,3},{3,2},{4,5},{5,4},{6,7},{7,6},{8,9},{9,8},{10,11... | collective-permute-start | bytes 1572872 | tf_op jit(solution)/shard_map/ppermute | solution.py:238
  16.2 12.2 %collective-permute-start.2 = (bf16[64,4096]{1,0:T(8,128)(2,1)S(1)}, bf16[64,4096]{1,0:T(8,128)(2,1)S(1)}, u32[]{:S(2)}, u32[]{:S(2)}) collective-permute-start(bf16[64,4096]{1,0:T(8,128)(2,1)S(1)} %bitcast_select_fusion), channel_id=1, source_target_pairs={{0,2},{2,0},{4,6},{6,4},{1,3},{3,1},{5,7},{7,5},{8,10},{10,8},{12,... | collective-permute-start | bytes 1572872 | tf_op jit(solution)/shard_map/ppermute | solution.py:238
  17.8 9.1 %collective-permute-start.16 = (bf16[64,1024]{1,0:T(8,128)(2,1)S(1)}, bf16[64,1024]{1,0:T(8,128)(2,1)S(1)}, u32[]{:S(2)}, u32[]{:S(2)}) collective-permute-start(bf16[64,1024]{1,0:T(8,128)(2,1)S(1)} %get-tuple-element.88), channel_id=1, source_target_pairs={{0,24},{8,16},{16,8},{24,0},{1,25},{9,17},{17,9},{25,1},{2,26},{10... | collective-permute-start | bytes 393224 | tf_op jit(solution)/shard_map/ppermute | solution.py:238
  22.8 13.8 %collective-permute-start.9 = (bf16[4,128,1024]{2,1,0:T(8,128)(2,1)S(1)}, bf16[4,128,1024]{2,1,0:T(8,128)(2,1)S(1)}, u32[]{:S(2)}, u32[]{:S(2)}) collective-permute-start(bf16[4,128,1024]{2,1,0:T(8,128)(2,1)S(1)} %pad_maximum_fusion.5), channel_id=1, source_target_pairs={{0,8},{8,16},{16,24},{24,0},{1,9},{9,17},{17,25},{25,1},{2,10},{10... | collective-permute-start | bytes 3145736 | tf_op jit(solution)/shard_map/ppermute | solution.py:234
  28.4 24.9 %collective-permute-start.4 = (bf16[64,4096]{1,0:T(8,128)(2,1)S(1)}, bf16[64,4096]{1,0:T(8,128)(2,1)S(1)}, u32[]{:S(2)}, u32[]{:S(2)}) collective-permute-start(bf16[64,4096]{1,0:T(8,128)(2,1)S(1)} %bitcast_select_fusion), channel_id=1, source_target_pairs={{0,4},{2,6},{4,0},{6,2},{1,5},{3,7},{5,1},{7,3},{8,12},{10,14},{12... | collective-permute-start | bytes 1572872 | tf_op jit(solution)/shard_map/ppermute | solution.py:238
  30.8 11.0 %collective-permute-start.3 = (bf16[64,4096]{1,0:T(8,128)(2,1)S(1)}, bf16[64,4096]{1,0:T(8,128)(2,1)S(1)}, u32[]{:S(2)}, u32[]{:S(2)}) collective-permute-start(bf16[64,4096]{1,0:T(8,128)(2,1)S(1)} %collective-permute-done.2), channel_id=1, source_target_pairs={{0,1},{1,0},{2,3},{3,2},{4,5},{5,4},{6,7},{7,6},{8,9},{9,8},{10,11... | collective-permute-start | bytes 1572872 | tf_op jit(solution)/shard_map/ppermute | solution.py:238
  36.9 22.5 %collective-permute-start.10 = (bf16[128,1024]{1,0:T(8,128)(2,1)S(1)}, bf16[128,1024]{1,0:T(8,128)(2,1)S(1)}, u32[]{:S(2)}, u32[]{:S(2)}) collective-permute-start(bf16[128,1024]{1,0:T(8,128)(2,1)S(1)} %get-tuple-element.78), channel_id=1, source_target_pairs={{0,2},{2,0},{4,6},{6,4},{1,3},{3,1},{5,7},{7,5},{8,10},{10,8},{12,... | collective-permute-start | bytes 786440 | tf_op jit(solution)/shard_map/ppermute | solution.py:238
  53.4 23.3 %collective-permute-start.11 = (bf16[128,1024]{1,0:T(8,128)(2,1)S(1)}, bf16[128,1024]{1,0:T(8,128)(2,1)S(1)}, u32[]{:S(2)}, u32[]{:S(2)}) collective-permute-start(bf16[128,1024]{1,0:T(8,128)(2,1)S(1)} %get-tuple-element.27), channel_id=1, source_target_pairs={{0,4},{2,6},{4,0},{6,2},{1,5},{3,7},{5,1},{7,3},{8,12},{10,14},{12... | collective-permute-start | bytes 786440 | tf_op jit(solution)/shard_map/ppermute | solution.py:238
  53.4 19.6 %collective-permute-start.6 = (bf16[64,4096]{1,0:T(8,128)(2,1)S(1)}, bf16[64,4096]{1,0:T(8,128)(2,1)S(1)}, u32[]{:S(2)}, u32[]{:S(2)}) collective-permute-start(bf16[64,4096]{1,0:T(8,128)(2,1)S(1)} %collective-permute-done.4), channel_id=1, source_target_pairs={{0,2},{2,0},{4,6},{6,4},{1,3},{3,1},{5,7},{7,5},{8,10},{10,8},{12,... | collective-permute-start | bytes 1572872 | tf_op jit(solution)/shard_map/ppermute | solution.py:238
  58.0 18.4 %collective-permute-start.5 = (bf16[64,4096]{1,0:T(8,128)(2,1)S(1)}, bf16[64,4096]{1,0:T(8,128)(2,1)S(1)}, u32[]{:S(2)}, u32[]{:S(2)}) collective-permute-start(bf16[64,4096]{1,0:T(8,128)(2,1)S(1)} %collective-permute-done.4), channel_id=1, source_target_pairs={{0,1},{1,0},{2,3},{3,2},{4,5},{5,4},{6,7},{7,6},{8,9},{9,8},{10,11... | collective-permute-start | bytes 1572872 | tf_op jit(solution)/shard_map/ppermute | solution.py:238
  68.9 30.5 %collective-permute-start.13 = (bf16[2,256,1024]{2,1,0:T(8,128)(2,1)S(1)}, bf16[2,256,1024]{2,1,0:T(8,128)(2,1)}, u32[]{:S(2)}, u32[]{:S(2)}) collective-permute-start(bf16[2,256,1024]{2,1,0:T(8,128)(2,1)S(1)} %bitcast.145), channel_id=1, source_target_pairs={{0,8},{8,0},{16,24},{24,16},{1,9},{9,1},{17,25},{25,17},{2,10},{10... | collective-permute-start | bytes 3145736 | tf_op jit(solution)/shard_map/ppermute | solution.py:238
  70.4 40.3 %collective-permute-start.21 = (bf16[2,256,1024]{2,1,0:T(8,128)(2,1)S(1)}, bf16[2,256,1024]{2,1,0:T(8,128)(2,1)}, u32[]{:S(2)}, u32[]{:S(2)}) collective-permute-start(bf16[2,256,1024]{2,1,0:T(8,128)(2,1)S(1)} %bitcast.146), channel_id=1, source_target_pairs={{0,16},{8,24},{16,0},{24,8},{1,17},{9,25},{17,1},{25,9},{2,18},{10... | collective-permute-start | bytes 3145736 | tf_op jit(solution)/shard_map/ppermute | solution.py:238
  73.0 8.4 %collective-permute-start.12 = (bf16[128,1024]{1,0:T(8,128)(2,1)S(1)}, bf16[128,1024]{1,0:T(8,128)(2,1)S(1)}, u32[]{:S(2)}, u32[]{:S(2)}) collective-permute-start(bf16[128,1024]{1,0:T(8,128)(2,1)S(1)} %get-tuple-element.28), channel_id=1, source_target_pairs={{0,6},{2,4},{4,2},{6,0},{1,7},{3,5},{5,3},{7,1},{8,14},{10,12},{12... | collective-permute-start | bytes 786440 | tf_op jit(solution)/shard_map/ppermute | solution.py:238
  76.4 11.9 %collective-permute-start.7 = (bf16[64,4096]{1,0:T(8,128)(2,1)S(1)}, bf16[64,4096]{1,0:T(8,128)(2,1)S(1)}, u32[]{:S(2)}, u32[]{:S(2)}) collective-permute-start(bf16[64,4096]{1,0:T(8,128)(2,1)S(1)} %collective-permute-done.6), channel_id=1, source_target_pairs={{0,1},{1,0},{2,3},{3,2},{4,5},{5,4},{6,7},{7,6},{8,9},{9,8},{10,11... | collective-permute-start | bytes 1572872 | tf_op jit(solution)/shard_map/ppermute | solution.py:238
  93.9 32.7 %collective-permute-start.8 = (bf16[512,1024]{1,0:T(8,128)(2,1)}, bf16[512,1024]{1,0:T(8,128)(2,1)}, u32[]{:S(2)}, u32[]{:S(2)}) collective-permute-start(bf16[512,1024]{1,0:T(8,128)(2,1)} %pad_maximum_fusion.4), channel_id=1, source_target_pairs={{0,8},{8,0},{16,24},{24,16},{1,9},{9,1},{17,25},{25,17},{2,10},{10... | collective-permute-start | bytes 3145736 | tf_op jit(solution)/shard_map/ppermute | solution.py:238
  96.3 15.0 %collective-permute-start.18 = (bf16[2,64,1024]{2,1,0:T(8,128)(2,1)S(1)}, bf16[2,64,1024]{2,1,0:T(8,128)(2,1)}, u32[]{:S(2)}, u32[]{:S(2)}) collective-permute-start(bf16[2,64,1024]{2,1,0:T(8,128)(2,1)S(1)} %pad_maximum_fusion.14), channel_id=1, source_target_pairs={{0,4},{2,6},{4,0},{6,2},{1,5},{3,7},{5,1},{7,3},{8,12},{10,14},{12... | collective-permute-start | bytes 786440 | tf_op jit(solution)/shard_map/ppermute | solution.py:238
  108.9 20.0 %collective-permute-start.14 = (bf16[2,256,1024]{2,1,0:T(8,128)(2,1)S(1)}, bf16[2,256,1024]{2,1,0:T(8,128)(2,1)}, u32[]{:S(2)}, u32[]{:S(2)}) collective-permute-start(bf16[2,256,1024]{2,1,0:T(8,128)(2,1)S(1)} %bitcast.147), channel_id=1, source_target_pairs={{0,8},{8,0},{16,24},{24,16},{1,9},{9,1},{17,25},{25,17},{2,10},{10... | collective-permute-start | bytes 3145736 | tf_op jit(solution)/shard_map/ppermute | solution.py:238
  109.0 24.5 %collective-permute-start.22 = (bf16[2,256,1024]{2,1,0:T(8,128)(2,1)S(1)}, bf16[2,256,1024]{2,1,0:T(8,128)(2,1)}, u32[]{:S(2)}, u32[]{:S(2)}) collective-permute-start(bf16[2,256,1024]{2,1,0:T(8,128)(2,1)S(1)} %bitcast.148), channel_id=1, source_target_pairs={{0,16},{8,24},{16,0},{24,8},{1,17},{9,25},{17,1},{25,9},{2,18},{10... | collective-permute-start | bytes 3145736 | tf_op jit(solution)/shard_map/ppermute | solution.py:238
  111.2 12.7 %collective-permute-start.19 = (bf16[2,64,1024]{2,1,0:T(8,128)(2,1)}, bf16[2,64,1024]{2,1,0:T(8,128)(2,1)S(1)}, u32[]{:S(2)}, u32[]{:S(2)}) collective-permute-start(bf16[2,64,1024]{2,1,0:T(8,128)(2,1)} %collective-permute-done.18), channel_id=1, source_target_pairs={{0,2},{2,0},{4,6},{6,4},{1,3},{3,1},{5,7},{7,5},{8,10},{10,8},{12,... | collective-permute-start | bytes 786440 | tf_op jit(solution)/shard_map/ppermute | solution.py:238
  118.4 30.7 %collective-permute-start.23 = (bf16[2,256,1024]{2,1,0:T(8,128)(2,1)}, bf16[2,256,1024]{2,1,0:T(8,128)(2,1)S(1)}, u32[]{:S(2)}, u32[]{:S(2)}) collective-permute-start(bf16[2,256,1024]{2,1,0:T(8,128)(2,1)} %collective-permute-done.21), channel_id=1, source_target_pairs={{0,8},{8,0},{16,24},{24,16},{1,9},{9,1},{17,25},{25,17},{2,10},{10... | collective-permute-start | bytes 3145736 | tf_op jit(solution)/shard_map/ppermute | solution.py:238
  126.4 25.5 %collective-permute-start.20 = (bf16[4,2,64,1024]{3,2,1,0:T(8,128)(2,1)}, bf16[4,2,64,1024]{3,2,1,0:T(8,128)(2,1)S(1)}, u32[]{:S(2)}, u32[]{:S(2)}) collective-permute-start(bf16[4,2,64,1024]{3,2,1,0:T(8,128)(2,1)} %copy.39), channel_id=1, source_target_pairs={{0,1},{1,0},{2,3},{3,2},{4,5},{5,4},{6,7},{7,6},{8,9},{9,8},{10,11... | collective-permute-start | bytes 3145736 | tf_op jit(solution)/shard_map/ppermute | solution.py:238
  128.9 20.1 %collective-permute-start.25 = (f32[15,1024]{1,0:T(8,128)S(1)}, f32[15,1024]{1,0:T(8,128)S(1)}, u32[]{:S(2)}, u32[]{:S(2)}) collective-permute-start(f32[15,1024]{1,0:T(8,128)S(1)} %select_maximum_fusion), channel_id=1, source_target_pairs={{0,16},{8,24},{16,0},{24,8},{1,17},{9,25},{17,1},{25,9},{2,18},{10... | collective-permute-start | bytes 184328 | tf_op jit(solution)/shard_map/ppermute | solution.py:238
  133.5 23.5 %collective-permute-start.24 = (bf16[2,256,1024]{2,1,0:T(8,128)(2,1)}, bf16[2,256,1024]{2,1,0:T(8,128)(2,1)S(1)}, u32[]{:S(2)}, u32[]{:S(2)}) collective-permute-start(bf16[2,256,1024]{2,1,0:T(8,128)(2,1)} %collective-permute-done.22), channel_id=1, source_target_pairs={{0,8},{8,0},{16,24},{24,16},{1,9},{9,1},{17,25},{25,17},{2,10},{10... | collective-permute-start | bytes 3145736 | tf_op jit(solution)/shard_map/ppermute | solution.py:238
  (26 other events, 200.3 us)
